TPU v7x, 32 devices: a whole 2x2x4 slice. The times are simulated.
32 devices in a mesh: fold: 4 (over x, core), tile: 8 (over z, y).
Axes of the slice: x: 2, y: 2, z: 4, core: 2. Of those that a mesh axis runs over, the one named last changes fastest.
Arguments:
- design: bfloat16 [8192, 8192], P('fold', 'tile'), may hold values from -0.0625 to 0.0625
- weights: float32 [8192], P('fold'), may hold values from 0.2 to 5
- response: float32 [8192], P('fold'), may hold values from -6 to 6
- fold_of: int32 [32], P('fold'), may hold values from 0 to 7, as said below
- smoothing: float32 [128], P('tile'), may hold values from 0.05 to 1
Outputs:
- complement: float32 [8, 8192, 8192], P('fold', 'tile')
- complement_rhs: float32 [8, 8192], P('fold', 'tile')
Inputs may be any that keep to these rules, and one draw needn't show every extreme that they name: `fold_of`: the slabs of rows g * 2048 to (g + 1) * 2048 - 1 carry only fold ids g * 2 to (g + 1) * 2 - 1, and each of these appears on at least one of those slabs.
All inputs are finite; a program needn't handle non-finite values.
Results may differ from a plain program's by a relative error of at most 0.0029.
Values may be sent and summed in bfloat16 or wider, within the bound.
A program may use at most 512 MiB of HBM per device.

v0:
```python
import jax
import jax.numpy as jnp
from jax import lax
from jax.sharding import PartitionSpec as P

FOLDS = 8
TERM = 64


def second_differences(width):
    rows = lax.broadcasted_iota(jnp.int32, (width - 2, width), 0)
    cols = lax.broadcasted_iota(jnp.int32, (width - 2, width), 1)
    diffs = (
        jnp.where(cols == rows, 1.0, 0.0)
        + jnp.where(cols == rows + 1, -2.0, 0.0)
        + jnp.where(cols == rows + 2, 1.0, 0.0)
    )
    diffs = diffs.astype(jnp.float32)
    return jnp.dot(
        diffs.T, diffs, precision=lax.Precision.HIGHEST, preferred_element_type=jnp.float32
    )


def body(design, weights, response, fold_of, smoothing):
    rows, block = design.shape
    slab_count = fold_of.shape[0]
    slab_rows = rows // slab_count
    me_tile = lax.axis_index("tile")
    held = FOLDS // lax.axis_size("fold")
    first_fold = lax.axis_index("fold") * held
    root_w = jnp.sqrt(weights)
    rooted = (design.astype(jnp.float32) * root_w[:, None]).astype(jnp.bfloat16)
    target = root_w * response
    member = (fold_of[:, None] == (first_fold + jnp.arange(held, dtype=jnp.int32))[None, :]).astype(
        jnp.float32
    )
    left = rooted.reshape(slab_count, slab_rows, block)
    slab_rhs = jnp.einsum(
        "sr,src->sc",
        target.reshape(slab_count, slab_rows),
        left.astype(jnp.float32),
        precision=lax.Precision.HIGHEST,
    )
    rhs_fold = jnp.einsum("sf,sc->fc", member, slab_rhs, precision=lax.Precision.HIGHEST)
    piece = lax.all_gather(rooted, "tile", axis=1, tiled=True)
    right = piece.reshape(slab_count, slab_rows, piece.shape[1])
    per_slab = jnp.einsum("src,srk->sck", left, right, preferred_element_type=jnp.float32)
    grams = jnp.einsum("sf,sck->fck", member, per_slab, precision=lax.Precision.HIGHEST)
    total_grams, total_rhs = lax.psum((jnp.sum(grams, axis=0), jnp.sum(rhs_fold, axis=0)), "fold")
    complement = total_grams[None] - grams
    complement_rhs = total_rhs[None] - rhs_fold
    penalty = jnp.kron(jnp.diag(smoothing), second_differences(TERM))
    column = me_tile * block
    current = lax.dynamic_slice_in_dim(complement, column, block, 2)
    complement = lax.dynamic_update_slice_in_dim(complement, current + penalty[None], column, 2)
    return (complement, complement_rhs)


def solution(mesh):
    in_specs = (P("fold", "tile"), P("fold"), P("fold"), P("fold"), P("tile"))
    out_specs = (P("fold", "tile", None), P("fold", "tile"))
    return jax.shard_map(body, mesh=mesh, in_specs=in_specs, out_specs=out_specs, check_vma=False)
```

profile of v0, /device:TPU:0, one launch (start us, length us, event | category | flops | bytes accessed | tf_op | source)
XLA Modules:
  0.0 2042.9 jit_solution(6480248486243621836)
XLA Ops:
  7.2 0.0 all-gather.2.cloned.1.call-start
  7.2 1.3 sqrt_multiply_fusion
  8.5 5.0 multiply_convert_fusion
  13.5 0.0 all-gather.2.cloned.1.call-update
  13.5 0.0 all-reduce.2.cloned.1.call-start
  13.6 640.5 %all-gather.2.cloned.1.call-done = bf16[2048,8192]{1,0:T(8,128)(2,1)} async-done(((bf16[2048,1024]{1,0:T(8,128)(2,1)}), bf16[2048,8192]{1,0:T(8,128)(2,1)}) %all-gather.2.cloned.1.call-update) | async-done | bytes 33554448 | tf_op jit(solution)/shard_map/all_gather | solution.py:45
  654.1 0.0 copy-start.2
  654.1 102.1 %fusion.27 = f32[8,1024,8192]{2,1,0:T(8,128)} fusion(bf16[8,256,1024]{2,1,0:T(8,128)(2,1)} %bitcast.21, bf16[8,256,8192]{2,1,0:T(8,128)(2,1)} %bitcast.23), kind=kOutput, calls=%fused_computation.41 | convolution fusion | flops 34359738368 | bytes 306184192 | tf_op jit(solution)/shard_map/src,srk->sck/dot_general | solution.py:47
  756.2 0.0 copy-done.2
  756.2 599.5 %fusion.25 = (f32[1024,8192]{1,0:T(8,128)}, f32[2,1024,8192]{2,0,1:T(2,128)}) fusion(f32[8,1024,8192]{2,1,0:T(8,128)} %fusion.27, s32[8]{0:T(128)S(1)} %copy-done.2, s32[2]{0:T(128)S(1)} %iota_add_fusion.2), kind=kOutput, calls=%fused_computation.39 | convolution fusion | flops 1619001344 | bytes 369098784 | tf_op jit(solution)/shard_map/sf,sck->fck/dot_general | solution.py:48
  1355.7 0.0 copy-start.1
  1355.7 0.0 copy-start
  1355.7 0.0 all-reduce.2.cloned.1.call-update
  1355.8 0.6 copy-done.1
  1356.4 0.1 fusion.16
  1356.4 0.3 fusion.5
  1356.8 4.1 broadcast_multiply_fusion
  1360.8 7.9 mul.51
  1368.7 0.0 copy-done
  1368.7 4.0 fusion.28
  1372.8 0.2 fusion.26
  1373.0 7.0 psum.15
  1380.0 0.6 broadcast_subtract_fusion.1
  1380.6 533.5 %all-reduce.2.cloned.1.call-done = f32[1024,8192]{1,0:T(8,128)} async-done(((f32[1024,8192]{1,0:T(8,128)}), f32[1024,8192]{1,0:T(8,128)}) %all-reduce.2.cloned.1.call-update) | async-done | bytes 33554448 | tf_op jit(solution)/shard_map/psum | solution.py:49
  1914.1 54.0 %broadcast_subtract_fusion = f32[2,1024,8192]{2,0,1:T(2,128)} fusion(f32[2,1024,8192]{2,0,1:T(2,128)} %get-tuple-element.7, f32[1024,8192]{1,0:T(8,128)} %all-reduce.2.cloned.1.call-done), kind=kLoop, calls=%fused_computation.2 | loop fusion | flops 16777216 | bytes 167772160 | tf_op jit(solution)/shard_map/sub | solution.py:50
  1968.1 11.5 add_dynamic-update-slice_fusion
  1979.6 56.4 %copy.7 = f32[2,1024,8192]{2,1,0:T(8,128)} copy(f32[2,1024,8192]{2,0,1:T(2,128)} %add_dynamic-update-slice_fusion) | data formatting | bytes 134217728
  (2 shorter events, 0.0 us)
Async XLA Ops:
  7.2 646.9 %all-gather.2.cloned.1.call-start = ((), (), s32[]{:S(2)}) async-start(), calls=%async_computation | async-start | bytes 37748736 | tf_op jit(solution)/shard_map/all_gather | solution.py:45
  13.5 1900.6 %all-reduce.2.cloned.1.call-start = ((), (), s32[]{:S(2)}) async-start(), calls=%async_computation.1 | async-start | bytes 67108864 | tf_op jit(solution)/shard_map/psum | solution.py:49
  654.1 102.1 %copy-start.2 = (s32[8]{0:T(128)S(1)}, s32[8]{0:T(128)}, u32[]{:S(2)}) copy-start(s32[8]{0:T(128)} %param.8) | copy-start | bytes 100
  1355.7 0.7 copy-start.1
  1355.7 13.0 copy-start
Sparse Core Ops, SparseCore 0:
  13.6 640.4 all-gather.1
  1355.9 558.2 all-reduce.1
where the time goes:
time: 2040 us
  waiting for transfers between devices  1170 us (57%)
  matrix products  706 us (35%)
  other arithmetic  76.5 us (4%)
  local copies, waits for them, and re-layouts  65 us (3%)
    all_gather x1, waiting for transfers between devices, body(): piece = lax.all_gather(rooted, 'tile', axis=1, tiled=True)  641 us
    dot_general x1, matrix products, body(): jnp.einsum('sf,sck->fck', member, per_slab, precision=lax.Precision.HIGHEST)  600 us
    psum x1, waiting for transfers between devices, body(): lax.psum((jnp.sum(grams, axis=0), jnp.sum(rhs_fold, axis=0)), 'fold')  533 us
    dot_general x1, matrix products, body(): jnp.einsum('src,srk->sck', left, right, preferred_element_type=jnp.float32)  102 us
    unnamed x7, local copies, waits for them, and re-layouts  57.1 us
    sub x1, other arithmetic, body(): complement = total_grams[None] - grams  54 us
  transfers between devices with their start and end apart: 2, of which 2 were waited for; matrix products, arithmetic and copies ran while one was open for 1% of the time, Pallas kernels for 0%

commit v1 on v0

v1 whole, which is shorter than its diff:
```python
import functools

import jax
import jax.numpy as jnp
from jax import lax
from jax.experimental import pallas as pl
from jax.experimental.pallas import tpu as pltpu
from jax.sharding import PartitionSpec as P

FOLDS = 8
TERM = 64
MESH = pl.DeviceIdType.MESH
SLOTS = 4


def second_differences(width):
    rows = lax.broadcasted_iota(jnp.int32, (width - 2, width), 0)
    cols = lax.broadcasted_iota(jnp.int32, (width - 2, width), 1)
    diffs = (
        jnp.where(cols == rows, 1.0, 0.0)
        + jnp.where(cols == rows + 1, -2.0, 0.0)
        + jnp.where(cols == rows + 2, 1.0, 0.0)
    )
    diffs = diffs.astype(jnp.float32)
    return jnp.dot(
        diffs.T, diffs, precision=lax.Precision.HIGHEST, preferred_element_type=jnp.float32
    )


def kernel(
    tiles, x_ref, mask_ref, target_ref, pen_ref, out_ref, crhs_ref,
    g, left, left_a, grams, rs_send, rs_recv, x_send, x_recv, ag_send, ag_recv,
    rhs, rhs_recv,
    in_sem, ring_send, ring_recv, rs_ss, rs_rs, x_ss, x_rs, ag_ss, ag_rs, out_sem,
    rhs_ss, rhs_rs,
):
    units = 2 * tiles
    depth, wide = g.shape[1], g.shape[2]
    block = 2 * wide
    half = block // 2
    sub_rows = depth // 2
    me = lax.axis_index("tile")
    fold = lax.axis_index("fold")
    core = fold % 2
    mate = fold + 1 - 2 * core
    across = (fold + 2) % 4
    place = (1 - me % 2) * (me // 2) + (me % 2) * (tiles - 1 - me // 2)

    def tile_at(position):
        position = position % tiles
        up = (position < tiles // 2).astype(jnp.int32)
        return up * (2 * position) + (1 - up) * (2 * (tiles - 1 - position) + 1)

    right = tile_at(place + 1)
    left_tile = tile_at(place + tiles - 1)
    neighbours = (right, left_tile)

    barrier = pltpu.get_barrier_semaphore()
    for device in ({"tile": right}, {"tile": left_tile}, {"fold": mate}, {"fold": across}):
        pl.semaphore_signal(barrier, inc=1, device_id=device, device_id_type=MESH)

    def load(side):
        return pltpu.make_async_copy(
            x_ref.at[:, pl.ds(side * wide, wide)], g.at[side], in_sem.at[side]
        )

    load(0).start()
    load(1).start()
    pl.semaphore_wait(barrier, 4)

    def hop(step, side, sub):
        rows = pl.ds(pl.multiple_of(sub * sub_rows, sub_rows), sub_rows)
        source, there = 2 * step + side, 2 * step + 2 + side
        return pltpu.make_async_remote_copy(
            src_ref=g.at[source, rows],
            dst_ref=g.at[there, rows],
            send_sem=ring_send.at[source, sub],
            recv_sem=ring_recv.at[there, sub],
            device_id={"tile": neighbours[side]},
            device_id_type=MESH,
        )

    for side in range(2):
        load(side).wait()
        for sub in range(2):
            hop(0, side, sub).start()

    chunk = 256
    for side in range(2):
        @pl.loop(0, depth // chunk)
        def _(i):
            at = pl.multiple_of(i * chunk, chunk)
            turned = g[side, pl.ds(at, chunk), :].T
            left[side * wide:(side + 1) * wide, pl.ds(at, chunk)] = turned
            kept = turned.astype(jnp.float32) * mask_ref[:, pl.ds(at, chunk)]
            left_a[side * wide:(side + 1) * wide, pl.ds(at, chunk)] = kept.astype(jnp.bfloat16)

    whole = target_ref[...]
    high = whole.astype(jnp.bfloat16)
    rest = whole - high.astype(jnp.float32)
    middle = rest.astype(jnp.bfloat16)
    low = (rest - middle.astype(jnp.float32)).astype(jnp.bfloat16)
    for side in range(2):
        columns = g[side]
        parts = [
            jnp.dot(part, columns, preferred_element_type=jnp.float32)
            for part in (low, middle, high)
        ]
        rhs[0, :, side * wide:(side + 1) * wide] = (parts[0] + parts[1]) + parts[2]

    def rhs_copy(stage, device):
        return pltpu.make_async_remote_copy(
            src_ref=rhs.at[stage], dst_ref=rhs_recv.at[stage],
            send_sem=rhs_ss.at[stage], recv_sem=rhs_rs.at[stage],
            device_id=device, device_id_type=MESH,
        )

    rhs_copy(0, {"fold": mate}).start()
    rhs_copy(0, {"fold": mate}).wait()
    rhs[1] = rhs[0] + rhs_recv[0]
    rhs_copy(1, {"fold": across}).start()

    def scatter(unit):
        return pltpu.make_async_remote_copy(
            src_ref=rs_send.at[unit % 2], dst_ref=rs_recv.at[unit % SLOTS],
            send_sem=rs_ss.at[unit % 2], recv_sem=rs_rs.at[unit % SLOTS],
            device_id={"fold": mate}, device_id_type=MESH,
        )

    def cross(unit):
        return pltpu.make_async_remote_copy(
            src_ref=x_send.at[unit % 2], dst_ref=x_recv.at[unit % SLOTS],
            send_sem=x_ss.at[unit % 2], recv_sem=x_rs.at[unit % SLOTS],
            device_id={"fold": across}, device_id_type=MESH,
        )

    def share(unit):
        return pltpu.make_async_remote_copy(
            src_ref=ag_send.at[unit % 2], dst_ref=ag_recv.at[unit % SLOTS],
            send_sem=ag_ss.at[unit % 2], recv_sem=ag_rs.at[unit % SLOTS],
            device_id={"fold": mate}, device_id_type=MESH,
        )

    def store(unit):
        side, step = unit % 2, unit // 2
        owner = tile_at(place + tiles + (2 * side - 1) * step)
        column = pl.multiple_of(owner * block + side * wide, wide)
        return pltpu.make_async_copy(
            grams.at[unit % SLOTS], out_ref.at[:, :, pl.ds(column, wide)],
            out_sem.at[unit % SLOTS],
        )

    mine = pl.ds(pl.multiple_of(core * half, half), half)
    other = pl.ds(pl.multiple_of((1 - core) * half, half), half)

    def products(unit, rows):
        slot = unit % SLOTS
        columns = g[unit]
        both = jnp.dot(left[rows, :], columns, preferred_element_type=jnp.float32)
        first = jnp.dot(left_a[rows, :], columns, preferred_element_type=jnp.float32)
        grams[slot, 0, rows, :] = first.astype(jnp.bfloat16)
        grams[slot, 1, rows, :] = (both - first).astype(jnp.bfloat16)
        return both

    def turn(k, carry):
        @pl.when((k >= 1) & (k <= units - 2))
        def _():
            step, sub = (k + 1) // 2, (k + 1) % 2
            for side in range(2):
                hop(step - 1, side, sub).wait_recv()

                @pl.when(step < tiles - 1)
                def _():
                    hop(step, side, sub).start()

        @pl.when((k >= 4) & (k - 4 < units))
        def _():
            store(k - 4).wait()

        @pl.when((k >= 3) & (k - 3 < units))
        def _():
            unit = k - 3
            slot = unit % SLOTS
            share(unit).wait()

            def finish(rows, sums):
                total = sums.astype(jnp.float32)
                for held in range(2):
                    part = grams[slot, held, rows, :].astype(jnp.float32)
                    grams[slot, held, rows, :] = (total - part).astype(jnp.bfloat16)

            finish(mine, ag_send[unit % 2])
            finish(other, ag_recv[slot])

            @pl.when(unit < 2)
            def _():
                for piece in range(wide // 128):
                    rows = pl.ds(pl.multiple_of(unit * wide + piece * 128, 128), 128)
                    cols = slice(piece * 128, (piece + 1) * 128)
                    for held in range(2):
                        now = grams[slot, held, rows, cols].astype(jnp.float32)
                        grams[slot, held, rows, cols] = (now + pen_ref[rows, :]).astype(
                            jnp.bfloat16
                        )

            store(unit).start()

        @pl.when((k >= 2) & (k - 2 < units))
        def _():
            unit = k - 2
            cross(unit).wait()
            ag_send[unit % 2] = (
                x_send[unit % 2].astype(jnp.float32)
                + x_recv[unit % SLOTS].astype(jnp.float32)
            ).astype(jnp.bfloat16)
            share(unit).start()

        @pl.when((k >= 1) & (k - 1 < units))
        def _():
            unit = k - 1
            slot = unit % SLOTS
            scatter(unit).wait()
            own = grams[slot, 0, mine, :].astype(jnp.float32) + grams[
                slot, 1, mine, :
            ].astype(jnp.float32)
            x_send[unit % 2] = (own + rs_recv[slot].astype(jnp.float32)).astype(jnp.bfloat16)
            cross(unit).start()

        @pl.when(k < units)
        def _():
            rs_send[k % 2] = products(k, other).astype(jnp.bfloat16)
            scatter(k).start()
            products(k, mine)

        return carry

    lax.fori_loop(0, units + 4, turn, 0)

    rhs_copy(1, {"fold": across}).wait()
    sums = rhs[1] + rhs_recv[1]
    crhs_ref[...] = (sums[0:1] + sums[1:2]) - rhs[0]

    def drain(step, carry):
        for side in range(2):
            for sub in range(2):
                hop(step, side, sub).wait_send()
        return carry

    lax.fori_loop(0, tiles - 1, drain, 0)


def body(tiles, design, weights, response, fold_of, smoothing):
    depth, block = design.shape
    wide = block // 2
    half = block // 2
    slab_rows = depth // fold_of.shape[0]
    held = FOLDS // lax.axis_size("fold")
    first_fold = lax.axis_index("fold") * held
    root_w = jnp.sqrt(weights)
    rooted = (design.astype(jnp.float32) * root_w[:, None]).astype(jnp.bfloat16)
    target = root_w * response
    row_fold = jnp.repeat(fold_of - first_fold, slab_rows)
    mask = (row_fold == 0).astype(jnp.float32)[None, :]
    line = lax.broadcasted_iota(jnp.int32, (16, depth), 0)
    targets = jnp.where(line == row_fold[None, :], target[None, :], 0.0)
    term_row = jnp.repeat(smoothing, TERM)[:, None]
    pattern = jnp.tile(second_differences(TERM), (block // TERM, 2))
    spot = (lax.broadcasted_iota(jnp.int32, (block, 2 * TERM), 0) // TERM) % 2
    spot = spot == lax.broadcasted_iota(jnp.int32, (block, 2 * TERM), 1) // TERM
    pen = jnp.where(spot, term_row * pattern, 0.0)
    bf16, f32 = jnp.bfloat16, jnp.float32
    dma = pltpu.SemaphoreType.DMA
    vmem = pl.BlockSpec(memory_space=pltpu.VMEM)
    hbm = pl.BlockSpec(memory_space=pl.ANY)
    size = tiles * block
    compact, crhs = pl.pallas_call(
        functools.partial(kernel, tiles),
        out_shape=(
            jax.ShapeDtypeStruct((2, block, size), bf16),
            jax.ShapeDtypeStruct((16, block), f32),
        ),
        in_specs=[hbm, vmem, vmem, vmem],
        out_specs=(hbm, vmem),
        scratch_shapes=[
            pltpu.VMEM((2 * tiles, depth, wide), bf16),
            pltpu.VMEM((block, depth), bf16),
            pltpu.VMEM((block, depth), bf16),
            pltpu.VMEM((SLOTS, 2, block, wide), bf16),
            pltpu.VMEM((2, half, wide), bf16),
            pltpu.VMEM((SLOTS, half, wide), bf16),
            pltpu.VMEM((2, half, wide), bf16),
            pltpu.VMEM((SLOTS, half, wide), bf16),
            pltpu.VMEM((2, half, wide), bf16),
            pltpu.VMEM((SLOTS, half, wide), bf16),
            pltpu.VMEM((2, 16, block), f32),
            pltpu.VMEM((2, 16, block), f32),
            dma((2,)),
            dma((2 * tiles, 2)),
            dma((2 * tiles, 2)),
            dma((2,)),
            dma((SLOTS,)),
            dma((2,)),
            dma((SLOTS,)),
            dma((2,)),
            dma((SLOTS,)),
            dma((SLOTS,)),
            dma((2,)),
            dma((2,)),
        ],
        compiler_params=pltpu.CompilerParams(
            collective_id=0, has_side_effects=True, vmem_limit_bytes=63 * 2**20
        ),
        cost_estimate=pl.CostEstimate(
            flops=4 * depth * block * size, bytes_accessed=8 * block * size, transcendentals=0
        ),
    )(rooted, mask, targets, pen)
    return (compact.astype(f32), crhs[:2])


def solution(mesh):
    tiles = mesh.shape["tile"]
    in_specs = (P("fold", "tile"), P("fold"), P("fold"), P("fold"), P("tile"))
    out_specs = (P("fold", "tile", None), P("fold", "tile"))
    return jax.shard_map(
        functools.partial(body, tiles),
        mesh=mesh, in_specs=in_specs, out_specs=out_specs, check_vma=False,
    )
```

time: 2040 us -> 410 us (0.20)
  waiting for transfers between devices: 1170 us -> 0 us
  matrix products: 706 us -> 0.31 us
  Pallas kernels: 0 us -> 364 us
  local copies, waits for them, and re-layouts: 65 us -> 3.89 us
  other arithmetic: 76.5 us -> 40.3 us
    dot_general x4 -> x0, matrix products: 706 us -> none  [the longest x1 600 us: body(): jnp.einsum('sf,sck->fck', member, per_slab, precision=lax.Precision.HIGHEST)]
    all_gather x1 -> x0, waiting for transfers between devices: 641 us -> none  [body(): piece = lax.all_gather(rooted, 'tile', axis=1, tiled=True)]
    psum x1 -> x0, waiting for transfers between devices: 533 us -> none  [body(): lax.psum((jnp.sum(grams, axis=0), jnp.sum(rhs_fold, axis=0)), 'fold')]
    pallas_call x0 -> x1, Pallas kernels: none -> 364 us  [body(): pl.pallas_call(functools.partial(kernel, tiles), out_shape=(jax.ShapeDtyp...]
    unnamed x7 -> x4, local copies, waits for them, and re-layouts: 57.1 us -> 0.76 us
    sub x2 -> x0, other arithmetic: 54.6 us -> none  [the longest x1 54 us: body(): complement = total_grams[None] - grams]
    convert_element_type x0 -> x2, other arithmetic: none -> 32.3 us  [the longest x1 31.6 us: body(): return (compact.astype(f32), crhs[:2])]
  transfers between devices with their start and end apart: 2 -> 0, of which waited for: 2 -> 0; matrix products, arithmetic and copies ran while one was open for 1% -> 0% of each run, Pallas kernels for 0% -> 0%
where the time goes in v1:
time: 410 us
  Pallas kernels  364 us (89%)
  other arithmetic  40.3 us (10%)
    pallas_call x1, Pallas kernels, body(): pl.pallas_call(functools.partial(kernel, tiles), out_shape=(jax.ShapeDtyp...  364 us
    convert_element_type x1, other arithmetic, body(): return (compact.astype(f32), crhs[:2])  31.6 us

profile of v1, /device:TPU:0, one launch (start us, length us, event | category | flops | bytes accessed | tf_op | source)
XLA Modules:
  0.0 409.5 jit_solution(7065749504078900200)
XLA Ops:
  0.6 0.7 compare_convert_fusion
  1.3 0.1 broadcast_bitcast_fusion.1
  1.4 0.6 copy.7
  2.0 0.1 broadcast_bitcast_fusion
  2.1 0.7 broadcast_in_dim.45
  2.8 0.1 mul.28
  2.9 0.7 sqrt_multiply_fusion
  3.6 0.3 fusion.3
  3.9 0.7 fusion.2.target_ref
  4.6 0.4 tile.4
  5.0 0.6 tile.10
  5.6 1.7 multiply_select_fusion.pen_ref
  7.3 4.9 %multiply_convert_fusion.x_ref = bf16[2048,1024]{1,0:T(8,128)(2,1)} fusion(bf16[2048,1024]{1,0:T(8,128)(2,1)} %param.5, f32[2048]{0:T(1024)S(1)} %get-tuple-element.9), kind=kLoop, calls=%fused_computation | loop fusion | flops 6291456 | bytes 8396800 | tf_op jit(solution)/shard_map/convert_element_type | solution.py:260
  12.2 364.3 %shard_map.68 = (bf16[2,1024,8192]{2,1,0:T(8,128)(2,1)}, f32[16,1024]{1,0:T(8,128)}) custom-call(bf16[2048,1024]{1,0:T(8,128)(2,1)} %multiply_convert_fusion.x_ref, f32[1,2048]{1,0:T(1,128)} %bitcast.8, f32[16,2048]{1,0:T(8,128)} %fusion.2.target_ref, f32[1024,128]{1,0:T(8,128)} %multiply_select_fusion.pen_ref), custom_call_target="tpu_custom_call" | custom-call | flops 68719476736 | bytes 67108864 | tf_op jit(solution)/shard_map/pallas_call | solution.py:276
  376.5 1.4 slice.3
  377.9 31.6 %convert_element_type.27 = f32[2,1024,8192]{2,1,0:T(8,128)} convert(bf16[2,1024,8192]{2,1,0:T(8,128)(2,1)} %get-tuple-element.4) | non-fusion elementwise | flops 16777216 | bytes 100663296 | tf_op jit(solution)/shard_map/convert_element_type | solution.py:317
  (6 shorter events, 0.0 us)

commit v2 on v1

--- a/solution.py
+++ b/solution.py
@@ -177,6 +177,33 @@
         def _():
             store(k - 4).wait()
 
+        @pl.when((k >= 1) & (k - 1 < units))
+        def _():
+            unit = k - 1
+            slot = unit % SLOTS
+            scatter(unit).wait()
+            own = grams[slot, 0, mine, :].astype(jnp.float32) + grams[
+                slot, 1, mine, :
+            ].astype(jnp.float32)
+            x_send[unit % 2] = (own + rs_recv[slot].astype(jnp.float32)).astype(jnp.bfloat16)
+            cross(unit).start()
+
+        @pl.when(k < units)
+        def _():
+            rs_send[k % 2] = products(k, other).astype(jnp.bfloat16)
+            scatter(k).start()
+            products(k, mine)
+
+        @pl.when((k >= 2) & (k - 2 < units))
+        def _():
+            unit = k - 2
+            cross(unit).wait()
+            ag_send[unit % 2] = (
+                x_send[unit % 2].astype(jnp.float32)
+                + x_recv[unit % SLOTS].astype(jnp.float32)
+            ).astype(jnp.bfloat16)
+            share(unit).start()
+
         @pl.when((k >= 3) & (k - 3 < units))
         def _():
             unit = k - 3
@@ -204,33 +231,6 @@
                         )
 
             store(unit).start()
-
-        @pl.when((k >= 2) & (k - 2 < units))
-        def _():
-            unit = k - 2
-            cross(unit).wait()
-            ag_send[unit % 2] = (
-                x_send[unit % 2].astype(jnp.float32)
-                + x_recv[unit % SLOTS].astype(jnp.float32)
-            ).astype(jnp.bfloat16)
-            share(unit).start()
-
-        @pl.when((k >= 1) & (k - 1 < units))
-        def _():
-            unit = k - 1
-            slot = unit % SLOTS
-            scatter(unit).wait()
-            own = grams[slot, 0, mine, :].astype(jnp.float32) + grams[
-                slot, 1, mine, :
-            ].astype(jnp.float32)
-            x_send[unit % 2] = (own + rs_recv[slot].astype(jnp.float32)).astype(jnp.bfloat16)
-            cross(unit).start()
-
-        @pl.when(k < units)
-        def _():
-            rs_send[k % 2] = products(k, other).astype(jnp.bfloat16)
-            scatter(k).start()
-            products(k, mine)
 
         return carry
 

time: 410 us -> 408 us (level)
  no operation moved by 1% of the time
where the time goes in v2:
time: 408 us
  Pallas kernels  363 us (89%)
  other arithmetic  40.3 us (10%)
    pallas_call x1, Pallas kernels, body(): pl.pallas_call(functools.partial(kernel, tiles), out_shape=(jax.ShapeDtyp...  363 us
    convert_element_type x1, other arithmetic, body(): return (compact.astype(f32), crhs[:2])  31.6 us

profile of v2, /device:TPU:0, one launch (start us, length us, event | category | flops | bytes accessed | tf_op | source)
XLA Modules:
  0.0 408.2 jit_solution(13248330763876262327)
XLA Ops:
  0.6 0.7 compare_convert_fusion
  1.3 0.1 broadcast_bitcast_fusion.1
  1.4 0.6 copy.7
  2.0 0.1 broadcast_bitcast_fusion
  2.1 0.7 broadcast_in_dim.45
  2.8 0.1 mul.28
  2.9 0.7 sqrt_multiply_fusion
  3.6 0.3 fusion.3
  3.9 0.7 fusion.2.target_ref
  4.6 0.4 tile.4
  5.0 0.6 tile.10
  5.6 1.7 multiply_select_fusion.pen_ref
  7.3 4.9 %multiply_convert_fusion.x_ref = bf16[2048,1024]{1,0:T(8,128)(2,1)} fusion(bf16[2048,1024]{1,0:T(8,128)(2,1)} %param.5, f32[2048]{0:T(1024)S(1)} %get-tuple-element.9), kind=kLoop, calls=%fused_computation | loop fusion | flops 6291456 | bytes 8396800 | tf_op jit(solution)/shard_map/convert_element_type | solution.py:260
  12.2 363.0 %shard_map.68 = (bf16[2,1024,8192]{2,1,0:T(8,128)(2,1)}, f32[16,1024]{1,0:T(8,128)}) custom-call(bf16[2048,1024]{1,0:T(8,128)(2,1)} %multiply_convert_fusion.x_ref, f32[1,2048]{1,0:T(1,128)} %bitcast.8, f32[16,2048]{1,0:T(8,128)} %fusion.2.target_ref, f32[1024,128]{1,0:T(8,128)} %multiply_select_fusion.pen_ref), custom_call_target="tpu_custom_call" | custom-call | flops 68719476736 | bytes 67108864 | tf_op jit(solution)/shard_map/pallas_call | solution.py:276
  375.2 1.4 slice.3
  376.6 31.6 %convert_element_type.27 = f32[2,1024,8192]{2,1,0:T(8,128)} convert(bf16[2,1024,8192]{2,1,0:T(8,128)(2,1)} %get-tuple-element.4) | non-fusion elementwise | flops 16777216 | bytes 100663296 | tf_op jit(solution)/shard_map/convert_element_type | solution.py:317
  (6 shorter events, 0.0 us)
